TPU v7x, 256 devices: a whole 4x4x8 slice. The times are simulated.
256 devices in a mesh: seq: 64 (over x, y_lo, z), head: 2 (over core), dp: 2 (over y_hi).
Axes of the slice: x: 4, y: 4 (y_hi: 2, y_lo: 2; y = y_hi * 2 + y_lo), z: 8, core: 2. Of those that a mesh axis runs over, the one named last changes fastest.
Arguments:
- tokens: bfloat16 [24576, 1024], P(('dp', 'seq')), parts along dimension 0, may hold values from -6 to 6
- frame_order: int32 [128], P(('dp', 'seq')), parts along dimension 0, may hold values from 0 to 63, each once
- target_mask: int32 [128], P(('dp', 'seq')), parts along dimension 0, may hold values 0 or 1
- pose_norm: float32 [1024], replicated, may hold values from 0.25 to 1.75
- pose_qkv: bfloat16 [3, 1024, 1024], P(None, None, 'head'), may hold values from -0.1875 to 0.1875
- pose_out: bfloat16 [1024, 1024], P('head'), may hold values from -0.1875 to 0.1875
- camera_head: float32 [1024, 12], replicated, may hold values from -0.1875 to 0.1875
- ray_embed: float32 [6, 1024], replicated, may hold values from -2.5 to 2.5
- render_norm: float32 [1024], replicated, may hold values from 0.25 to 1.75
- render_qkv: bfloat16 [3, 1024, 1024], P(None, None, 'head'), as said below
- render_out: bfloat16 [1024, 1024], P('head'), may hold values from -0.1875 to 0.1875
Outputs:
- rendered: bfloat16 [24576, 1024], P(('dp', 'seq'), 'head'), parts along dimension 0
- cameras: float32 [128, 12], P(('dp', 'seq')), parts along dimension 0
There are 2 independent parts, one for each index of `dp`. A program takes and returns all parts, laid end to end along the dimension named above; an argument that names none is the same for every part. Nothing has to cross between parts.
Inputs may be any that keep to these rules, and one draw needn't show every extreme that they name: `frame_order`: each frame's time index once. `render_qkv`: entries of magnitude at most 9 / sqrt(1024).
All inputs are finite; a program needn't handle non-finite values. No bound on the sum of `target_mask` on one device may be relied on, other than what follows from the above.
Results may differ from a plain program's by a relative error of at most 0.023.
Values may be sent and summed in bfloat16 or wider, within the bound.
No kernel may reach another device: no remote copies, remote signals or barrier semaphores. Data moves between devices by JAX's collectives and lax.ppermute only.
A program may use at most 128 MiB of HBM per device.

v0:
```python
import functools

import jax
import jax.numpy as jnp
from jax import lax
from jax.experimental import pallas as pl
from jax.experimental.pallas import tpu as pltpu
from jax.sharding import Mesh
from jax.sharding import PartitionSpec as P

F32 = jnp.float32
BF16 = jnp.bfloat16
HEAD_DIM = 64
GRID = 32
ROWS = 192
WIDTH = 1024
HALF = 512
HEADS = 8
PAIRS = 4
GROUP = 8
RING = 4
TALL = 208
CAM = 12
FRAMES = 64
LOG2E = 1.4426950408889634
VMEM_LIMIT = 56 * 1024 * 1024
SMEM = pl.BlockSpec(memory_space=pltpu.SMEM)
VMEM = pl.BlockSpec(memory_space=pltpu.VMEM)


def split3(value):
    high = value.astype(BF16).astype(F32)
    rest = value - high
    mid = rest.astype(BF16).astype(F32)
    return high, mid, rest - mid


def mm(left, right):
    return jnp.dot(left, right, preferred_element_type=F32)


def mm_t(left, right):
    return lax.dot_general(left, right, (((1,), (1,)), ((), ())), preferred_element_type=F32)


def start_kernel(order_ref, mask_ref, tokens_ref, send_ref, near_ref, far_ref):
    tokens = tokens_ref[...].astype(F32)
    pooled = jnp.sum(tokens, axis=0, keepdims=True) * (1.0 / ROWS)
    pieces = [pooled[:, at * 128 : at * 128 + 128] for at in range(8)]
    index = lax.broadcasted_iota(jnp.int32, (8, 128), 0) * 128 + lax.broadcasted_iota(jnp.int32, (8, 128), 1)
    rate = jnp.exp(-4.0 * index.astype(F32) / WIDTH)
    wave = jnp.sin(order_ref[0].astype(F32) * rate)
    cam = (jnp.concatenate(pieces, axis=0) + wave).astype(BF16).astype(F32)
    send_ref[...] = jnp.broadcast_to(cam[None], send_ref.shape)
    kept = (tokens * (1 - mask_ref[0]).astype(F32)).astype(BF16)
    first = lax.axis_index("h") == 0
    near_ref[...] = jnp.where(first, kept[:, :HALF], kept[:, HALF:])
    far_ref[...] = jnp.where(first, kept[:, HALF:], kept[:, :HALF])


def start(order, mask, tokens):
    return pl.pallas_call(
        start_kernel,
        in_specs=[SMEM, SMEM, VMEM],
        out_specs=[VMEM] * 3,
        out_shape=[
            jax.ShapeDtypeStruct((FRAMES, 8, 128), F32),
            jax.ShapeDtypeStruct((ROWS, HALF), BF16),
            jax.ShapeDtypeStruct((ROWS, HALF), BF16),
        ],
        compiler_params=pltpu.CompilerParams(vmem_limit_bytes=VMEM_LIMIT),
        name="start",
    )(order, mask, tokens)


def pose_kernel(cam_ref, gain_ref, qkv_ref, out_ref, head_ref, cams_ref):
    cam = jnp.concatenate([cam_ref[:, at, :] for at in range(8)], axis=1)
    mean = jnp.mean(cam * cam, axis=-1, keepdims=True)
    normed = (cam * lax.rsqrt(mean + 1e-06) * gain_ref[...]).astype(BF16)
    query = mm(normed, qkv_ref[0]).astype(BF16)
    keys = mm(normed, qkv_ref[1]).astype(BF16)
    values = mm(normed, qkv_ref[2]).astype(BF16)
    lane_head = lax.broadcasted_iota(jnp.int32, (FRAMES, HALF), 1) >> 6
    stacked = jnp.concatenate(
        [jnp.where(lane_head == head, query, jnp.zeros_like(query)) for head in range(HEADS)], axis=0
    )
    scores = mm_t(stacked, keys) * (1.0 / HEAD_DIM**0.5)
    weights = jnp.exp(scores - jnp.max(scores, axis=-1, keepdims=True))
    total = jnp.sum(weights, axis=-1, keepdims=True)
    mixed = mm(weights.astype(BF16), values) / total
    picked = None
    for head in range(HEADS):
        rows = mixed[head * FRAMES : (head + 1) * FRAMES]
        picked = rows if picked is None else jnp.where(lane_head == head, rows, picked)
    partial = mm(picked.astype(BF16), out_ref[...]) + 0.5 * cam
    cams_ref[...] = lax.dot_general(
        partial,
        head_ref[...],
        (((1,), (1,)), ((), ())),
        precision=lax.Precision.HIGHEST,
        preferred_element_type=F32,
    )


def pose(cam_all, pose_norm, pose_qkv, pose_out, camera_head):
    return pl.pallas_call(
        pose_kernel,
        out_shape=jax.ShapeDtypeStruct((FRAMES, CAM), F32),
        compiler_params=pltpu.CompilerParams(vmem_limit_bytes=VMEM_LIMIT),
        name="pose",
    )(cam_all, pose_norm, pose_qkv, pose_out, camera_head)


def ray_rows(cams):
    frames = cams.shape[0]
    place_at = lax.broadcasted_iota(jnp.int32, (frames, ROWS), 1)
    across = ((place_at & (GRID - 1)).astype(F32) + 0.5) * (2.0 / GRID) - 1.0
    down = ((place_at >> 5).astype(F32) + 0.5) * (2.0 / GRID) - 1.0
    squashed = jnp.tanh(cams)

    def turn(which):
        return squashed[:, which : which + 1] * 0.3

    def place(which):
        return squashed[:, 9 + which : 10 + which] * 2.0

    one = (1.0 + turn(0)) * across + turn(1) * down + turn(2)
    two = turn(3) * across + (1.0 + turn(4)) * down + turn(5)
    three = turn(6) * across + turn(7) * down + (1.0 + turn(8))
    length = jnp.sqrt(one * one + two * two + three * three)
    u_one, u_two, u_three = one / length, two / length, three / length
    return (
        u_one,
        u_two,
        u_three,
        place(1) * u_three - place(2) * u_two,
        place(2) * u_one - place(0) * u_three,
        place(0) * u_two - place(1) * u_one,
    )


def prep_kernel(keys, queries, spots, cams_ref, more_ref, embed_ref, gain_ref, qkv_hbm, *refs):
    frames = [("k", offset) for group in keys for offset in group] + [("q",) + spot for group in queries for spot in group]
    arrays = 2 * (max(spot[0] for spot in spots) + 1)
    inputs = refs[:arrays]
    k_hbm, v_hbm, q_hbm, share_ref, own_ref = refs[arrays : arrays + 5]
    qkv_ref, block_buf, k_ref, v_ref, q_ref, sems, out_sems = refs[arrays + 5 :]
    sent = []

    def send(source, target):
        copy = pltpu.make_async_copy(source, target, out_sems.at[len(sent)])
        copy.start()
        sent.append(copy)

    at_x, at_y, at_z, core = (lax.axis_index(name) for name in ("x", "y", "z", "h"))
    other = 1 - core
    copies = []

    def fetch(source, target):
        copy = pltpu.make_async_copy(source, target, sems.at[len(copies)])
        copy.start()
        copies.append(copy)
        return copy

    matrices = ([1, 2] if keys else []) + ([0] if queries else [])
    weights = {
        which: [
            fetch(qkv_hbm.at[which, side], qkv_ref.at[which, pl.ds(at * HALF, HALF)])
            for at, side in enumerate((core, other))
        ]
        for which in matrices
    }
    waits = []
    for at, (array, plane) in enumerate(spots):
        pair = inputs[2 * array : 2 * array + 2]
        if plane is not None:
            pair = [ref.at[plane] for ref in pair]
        waits.append(
            [fetch(ref, block_buf.at[at, :, pl.ds(side * HALF, HALF)]) for side, ref in enumerate(pair)]
        )
    row = lax.broadcasted_iota(jnp.int32, (2 * GROUP, FRAMES), 0)
    key_frame = at_x * 16 + at_y * 8 + ((at_z - row) & 7)
    query_frame = ((at_x - row) & 3) * 16 + ((at_y - (row >> 2)) & 1) * 8 + at_z
    wanted = jnp.where(row < GROUP, key_frame, query_frame)
    pick = jnp.where(lax.broadcasted_iota(jnp.int32, (2 * GROUP, FRAMES), 1) == wanted, 1.0, 0.0)
    cams = jnp.dot(
        pick, cams_ref[...] + more_ref[...], precision=lax.Precision.HIGHEST, preferred_element_type=F32
    )
    rays = ray_rows(cams)
    zeros = jnp.zeros((2, ROWS), F32)
    embeds = []
    for side in (core, other):
        pad = jnp.zeros((2, HALF), F32)
        span = pl.ds(pl.multiple_of(side * HALF, HALF), HALF)
        high, mid, low = split3(jnp.concatenate([embed_ref[:, span], pad], axis=0))
        embeds.append(jnp.concatenate([high, mid, high, mid, low, high], axis=0).astype(BF16))
    embeds = jnp.concatenate(embeds, axis=1)
    gains = jnp.concatenate([gain_ref[core], gain_ref[other]], axis=1)

    def inputs_of(at):
        kind = frames[at]
        frame = kind[1] if kind[0] == "k" else GROUP + kind[2] * RING + kind[1]
        six = jnp.concatenate([ray[frame : frame + 1] for ray in rays] + [zeros], axis=0)
        high, mid, low = split3(six)
        stacked = jnp.concatenate([high, high, mid, mid, high, low], axis=0).astype(BF16)
        embedded = lax.dot_general(stacked, embeds, (((0,), (0,)), ((), ())), preferred_element_type=F32)
        return (block_buf[at].astype(F32) + embedded).astype(BF16)

    def normed(inputs):
        wide = inputs.astype(F32)
        factor = lax.rsqrt(jnp.sum(wide * wide, axis=-1, keepdims=True) * (1.0 / WIDTH) + 1e-06)
        return (wide * factor * gains).astype(BF16)

    def project(rows, which):
        return mm(rows, qkv_ref[which])

    own_ref[...] = cams[0:1]
    at = 0
    for group in list(keys) + list(queries):
        members = range(at, at + len(group))
        for member in members:
            for copy in waits[member]:
                copy.wait()
        raw = [inputs_of(member) for member in members]
        pair = jnp.concatenate([normed(part) for part in raw], axis=0)
        if frames[at][0] == "k":
            if at == 0:
                for copy in weights[1] + weights[2]:
                    copy.wait()
            span = slice(at * ROWS, (at + len(group)) * ROWS)
            k_ref[span, :] = project(pair, 1).astype(BF16)
            v_ref[span, :] = project(pair, 2).astype(BF16)
            rows = pl.ds(at * ROWS, len(group) * ROWS)
            send(k_ref.at[rows], k_hbm.at[rows])
            send(v_ref.at[rows], v_hbm.at[rows])
        else:
            if group is queries[0]:
                for copy in weights[0]:
                    copy.wait()
            query = (project(pair, 0) * (LOG2E / HEAD_DIM**0.5)).astype(BF16)
            for spot, (by_x, by_y) in enumerate(group):
                if (by_x, by_y) == (0, 0):
                    share_ref[...] = raw[spot][:, :HALF]
                held = at + spot - GROUP
                q_ref[held] = query[spot * ROWS : (spot + 1) * ROWS]
                send(q_ref.at[held], q_hbm.at[RING + ((at_x - by_x) & (RING - 1)) if by_y else by_x])
        at += len(group)
    for copy in sent:
        copy.wait()


def prep(keys, queries, cams, more, embed, gain, qkv, blocks):
    any_space = pl.BlockSpec(memory_space=pltpu.HBM)
    spots = []
    for array, value in enumerate(blocks):
        spots += [(array, None)] if value[0].ndim == 2 else [(array, plane) for plane in range(2)]
    count = len(spots)
    blocks = [item for value in blocks for item in value]
    wide = jax.ShapeDtypeStruct((GROUP * ROWS, HALF), BF16)
    shapes = [
        wide,
        wide,
        jax.ShapeDtypeStruct((GROUP, ROWS, HALF), BF16),
        jax.ShapeDtypeStruct((ROWS, HALF), BF16),
        jax.ShapeDtypeStruct((1, CAM), F32),
    ]
    return pl.pallas_call(
        functools.partial(prep_kernel, keys, queries, tuple(spots)),
        in_specs=[VMEM] * 4 + [any_space] * (1 + len(blocks)),
        out_specs=[any_space] * 3 + [VMEM] * 2,
        out_shape=shapes,
        scratch_shapes=[
            pltpu.VMEM((3, WIDTH, HALF), BF16),
            pltpu.VMEM((count, ROWS, WIDTH), BF16),
            pltpu.VMEM((GROUP * ROWS, HALF), BF16),
            pltpu.VMEM((GROUP * ROWS, HALF), BF16),
            pltpu.VMEM((GROUP, ROWS, HALF), BF16),
            pltpu.SemaphoreType.DMA((2 * count + 6,)),
            pltpu.SemaphoreType.DMA((2 * len(keys) + GROUP,)),
        ],
        compiler_params=pltpu.CompilerParams(vmem_limit_bytes=VMEM_LIMIT),
        name="prep",
    )(cams, more, embed, gain, qkv, *blocks)


def pack_levels(out_ref, index, compact):
    out_ref[index, ROWS:TALL, :] = jnp.zeros((TALL - ROWS, HALF), BF16)
    out_ref[index, ROWS:TALL, 0:ROWS] = compact[0:16].astype(BF16)
    out_ref[index, ROWS:TALL, 256 : 256 + ROWS] = compact[16:32].astype(BF16)


def attend_kernel(q_ref, k_ref, v_ref, *out_refs):
    lane = lax.broadcasted_iota(jnp.int32, (1, 128), 1)
    count = q_ref.shape[0]
    places = [(out_refs[0], at) for at in range(count)] if len(out_refs) < count else [(ref, 0) for ref in out_refs]
    ones = jnp.ones((k_ref.shape[0], 128), BF16)
    stat = None
    for pair in range(PAIRS):
        part = slice(pair * 128, pair * 128 + 128)
        query = jnp.concatenate([q_ref[at, :, part] for at in range(count)], axis=0)
        keys = k_ref[:, part]
        values = v_ref[:, part]
        joined = None
        for side in range(2):
            mine = (lane >> 6) == side
            scores = mm_t(jnp.where(mine, query, jnp.zeros_like(query)), keys)
            top = jnp.max(scores, axis=-1, keepdims=True)
            weights = jnp.exp2(scores - top).astype(BF16)
            extended = jnp.concatenate([jnp.where(mine, values, jnp.zeros_like(values)), ones], axis=1)
            both = mm(weights, extended)
            total = both[:, 128:]
            result = both[:, :128] / total
            joined = result if joined is None else joined + result
            level = top + jnp.log2(total)
            head = pair * 2 + side
            stat = level if stat is None else jnp.where((lane & 7) == head, level, stat)
        joined = joined.astype(BF16)
        for at, (ref, index) in enumerate(places):
            ref[index, 0:ROWS, part] = joined[at * ROWS : (at + 1) * ROWS]
    high, mid, low = split3(stat)
    packed = jnp.where(lane < 8, high, jnp.where(lane < 16, mid, jnp.where(lane < 24, low, 0.0))).astype(BF16)
    same = lax.broadcasted_iota(jnp.int32, (32, 128), 0) == lax.broadcasted_iota(jnp.int32, (32, 128), 1)
    pick = jnp.where(same, 1.0, 0.0).astype(BF16)
    for at, (ref, index) in enumerate(places):
        pack_levels(ref, index, mm_t(pick, packed[at * ROWS : (at + 1) * ROWS]))


def attend(query, keys, values, first, count, together):
    shape = (RING, TALL, HALF) if together else (1, TALL, HALF)
    spans = RING // count if together else 1
    outs = 1 if together else count
    block = (count if together else 1, TALL, HALF)
    return pl.pallas_call(
        attend_kernel,
        grid=(spans,),
        in_specs=[
            pl.BlockSpec((pl.Element(count), pl.Element(ROWS), pl.Element(HALF)), lambda i: (first + i * count, 0, 0)),
            VMEM,
            VMEM,
        ],
        out_specs=[pl.BlockSpec(block, lambda i: (i, 0, 0))] * outs,
        out_shape=[jax.ShapeDtypeStruct(shape, BF16)] * outs,
        compiler_params=pltpu.CompilerParams(vmem_limit_bytes=VMEM_LIMIT),
        name="attend",
    )(query, keys, values)


def join_parts(parts):
    row = lax.broadcasted_iota(jnp.int32, (32, HALF), 0)
    column = lax.broadcasted_iota(jnp.int32, (32, HALF), 1)
    spread = jnp.where(((row & 7) == (column >> 6)) & (row < 24), 1.0, 0.0).astype(BF16)
    levels = []
    for ref, index in parts:
        compact = jnp.concatenate(
            [ref[index, ROWS:TALL, 0:ROWS], ref[index, ROWS:TALL, 256 : 256 + ROWS]], axis=0
        )
        levels.append(
            lax.dot_general(compact, spread, (((0,), (0,)), ((), ())), preferred_element_type=F32)
        )
    top = levels[0]
    for level in levels[1:]:
        top = jnp.maximum(top, level)
    total = None
    mixed = None
    for (ref, index), level in zip(parts, levels):
        weight = jnp.exp2(level - top)
        value = weight * ref[index, 0:ROWS, :].astype(F32)
        total = weight if total is None else total + weight
        mixed = value if mixed is None else mixed + value
    return mixed / total, top, total


def join_kernel(parts_ref, out_ref):
    result, top, total = join_parts([(parts_ref, at) for at in range(RING)])
    out_ref[0, 0:ROWS, :] = result.astype(BF16)
    row = lax.broadcasted_iota(jnp.int32, (8, HALF), 0)
    column = lax.broadcasted_iota(jnp.int32, (8, HALF), 1)
    pick = jnp.where(row * HEAD_DIM == column, 1.0, 0.0).astype(BF16)
    pieces = [mm_t(pick, piece.astype(BF16)) for piece in split3(top + jnp.log2(total))]
    pack_levels(out_ref, 0, jnp.concatenate(pieces + [jnp.zeros((8, ROWS), F32)], axis=0))


def join(parts):
    return pl.pallas_call(
        join_kernel,
        out_shape=jax.ShapeDtypeStruct((1, TALL, HALF), BF16),
        compiler_params=pltpu.CompilerParams(vmem_limit_bytes=VMEM_LIMIT),
        name="join",
    )(parts)


def merge_kernel(out_ref, *refs):
    parts, (mine_ref, send_ref) = refs[:-2], refs[-2:]
    core = lax.axis_index("h")
    result, _, _ = join_parts([(ref, 0) for ref in parts])
    attended = result.astype(BF16)
    mine_ref[...] = mm(attended, out_ref[:, pl.ds(pl.multiple_of(core * HALF, HALF), HALF)])
    send_ref[...] = mm(attended, out_ref[:, pl.ds(pl.multiple_of((1 - core) * HALF, HALF), HALF)]).astype(BF16)


def merge(render_out, parts):
    return pl.pallas_call(
        merge_kernel,
        in_specs=[VMEM] * (1 + len(parts)),
        out_specs=[VMEM] * 2,
        out_shape=[
            jax.ShapeDtypeStruct((ROWS, HALF), F32),
            jax.ShapeDtypeStruct((ROWS, HALF), BF16),
        ],
        compiler_params=pltpu.CompilerParams(vmem_limit_bytes=VMEM_LIMIT),
        name="merge",
    )(render_out, *parts)


def shift(value, axis, size, by):
    return lax.ppermute(value, axis, [(at, (at + by) % size) for at in range(size)])


def local(
    tokens,
    frame_order,
    target_mask,
    pose_norm,
    pose_qkv,
    pose_out,
    camera_head,
    ray_embed,
    render_norm,
    render_qkv,
    render_out,
):
    send, near, far = start(frame_order, target_mask, tokens)

    def other(value):
        return shift(value, "h", 2, 1)

    def step_up(value):
        return shift(value, "z", 8, 1)

    def step_down(value):
        return shift(value, "z", 8, 7)

    tie = lax.optimization_barrier
    cam_all = lax.all_to_all(send, ("x", "y", "z"), 0, 0)
    up1, down1, across = step_up(near), step_down(near), shift(near, "y", 2, 1)
    opposite = shift(near, "z", 8, 4)
    cam_all, up1, down1, across = tie((cam_all, up1, down1, across))
    up2, down2 = step_up(up1), step_down(down1)
    planes = jnp.stack([near, across])
    side1, side3, side2 = (shift(planes, "x", 4, by) for by in (1, 3, 2))
    cams = pose(cam_all, pose_norm[None, :], pose_qkv, pose_out, camera_head.T)
    cams, up2, down2, opposite = tie((cams, up2, down2, opposite))
    more = other(cams)
    up3, down3 = step_up(up2), step_down(down2)
    more, up3, down3, side1, side3, side2 = tie((more, up3, down3, side1, side3, side2))
    gain = render_norm.reshape(2, 1, HALF)
    qkv = render_qkv.reshape(3, 2, HALF, HALF)

    def pair(value):
        return (value, other(value))

    own_pair = (near, far)
    key, val, query, share, own = prep(
        ((0, 1, 7, 2), (6, 4, 3, 5)),
        (((0, 0), (0, 1)), ((1, 0), (1, 1), (3, 0), (3, 1)), ((2, 0), (2, 1))),
        cams,
        more,
        ray_embed,
        gain,
        qkv,
        [own_pair]
        + [pair(value) for value in (up1, down1, up2, down2, opposite, up3, down3)]
        + [own_pair]
        + [pair(value) for value in (across, side1, side3, side2)],
    )
    far_parts = lax.all_to_all(attend(query, key, val, RING, 2, True)[0], "x", 0, 0)
    sides = [shift(part, "x", 4, -by) for by, part in zip((1, 2, 3), attend(query, key, val, 1, 3, False))]
    crossed = join(far_parts)
    query, crossed = tie((query, crossed))
    crossed = shift(crossed, "y", 2, 1)
    nearest = attend(query, key, val, 0, 1, False)
    mine, outgoing = merge(render_out, [*nearest, crossed, *sides])
    theirs = other(outgoing)
    rendered = (share.astype(F32) + (mine + theirs.astype(F32))).astype(BF16)
    return (rendered, own)


def solution(mesh):
    fine = Mesh(mesh.devices.reshape(4, 2, 8, 2, 2), ("x", "y", "z", "h", "dp"))
    rows = ("dp", "x", "y", "z")
    in_specs = (
        P(rows, None),
        P(rows),
        P(rows),
        P(),
        P(None, None, "h"),
        P("h", None),
        P(),
        P(),
        P(),
        P(None, None, "h"),
        P("h", None),
    )
    out_specs = (P(rows, "h"), P(rows, None))
    return jax.shard_map(local, mesh=fine, in_specs=in_specs, out_specs=out_specs, check_vma=False)
```

profile of v0, /device:TPU:1, one launch (start us, length us, event | category | flops | bytes accessed | tf_op | source)
XLA Modules:
  0.0 145.1 jit_solution(219248600941022300)
XLA Ops:
  1.9 2.0 %start.1 = (f32[64,8,128]{2,1,0:T(8,128)}, bf16[192,512]{1,0:T(8,128)(2,1)}, bf16[192,512]{1,0:T(8,128)(2,1)}) custom-call(s32[1]{0:T(128)S(6)} %copy.13.order_ref, s32[1]{0:T(128)S(6)} %copy.14.mask_ref, bf16[192,1024]{1,0:T(8,128)(2,1)} %tokens_ref.1), custom_call_target="tpu_custom_call" | custom-call | tf_op jit(solution)/shard_map/start/pallas_call | solution.py:62
  3.9 13.5 %all-to-all-start = ((f32[64,8,128]{2,1,0:T(8,128)}), f32[64,8,128]{2,1,0:T(8,128)S(1)}, u32[]{:S(2)}, u32[]{:S(2)}) async-start(f32[64,8,128]{2,1,0:T(8,128)} %get-tuple-element.31), calls=%async_computation | async-start | bytes 524288 | tf_op jit(solution)/shard_map/all_to_all | solution.py:444
  18.5 2.4 %collective-permute-start.1 = (bf16[192,512]{1,0:T(8,128)(2,1)}, bf16[192,512]{1,0:T(8,128)(2,1)S(1)}, u32[]{:S(2)}, u32[]{:S(2)}) collective-permute-start(bf16[192,512]{1,0:T(8,128)(2,1)} %get-tuple-element.32.refs_0_.refs_16_), channel_id=1, source_target_pairs={{0,28},{4,0},{8,4},{12,8},{16,12},{20,16},{24,20},{28,24},{1,29},{... | collective-permute-start | bytes 589832 | tf_op jit(solution)/shard_map/ppermute | solution.py:416
  20.9 4.2 %collective-permute-start.5 = (bf16[192,512]{1,0:T(8,128)(2,1)}, bf16[192,512]{1,0:T(8,128)(2,1)S(1)}, u32[]{:S(2)}, u32[]{:S(2)}) collective-permute-start(bf16[192,512]{1,0:T(8,128)(2,1)} %get-tuple-element.32.refs_0_.refs_16_), channel_id=1, source_target_pairs={{0,16},{4,20},{8,24},{12,28},{16,0},{20,4},{24,8},{28,12},{1,17},{... | collective-permute-start | bytes 589832 | tf_op jit(solution)/shard_map/ppermute | solution.py:416
  25.1 3.1 %collective-permute-done.1.refs_4_ = bf16[192,512]{1,0:T(8,128)(2,1)S(1)} collective-permute-done((bf16[192,512]{1,0:T(8,128)(2,1)}, bf16[192,512]{1,0:T(8,128)(2,1)S(1)}, u32[]{:S(2)}, u32[]{:S(2)}) %collective-permute-start.1) | collective-permute-done | bytes 196640 | tf_op jit(solution)/shard_map/ppermute | solution.py:416
  30.3 1.6 %collective-permute-start.4 = (bf16[192,512]{1,0:T(8,128)(2,1)S(1)}, bf16[192,512]{1,0:T(8,128)(2,1)S(1)}, u32[]{:S(2)}, u32[]{:S(2)}) collective-permute-start(bf16[192,512]{1,0:T(8,128)(2,1)S(1)} %collective-permute-done.1.refs_4_), channel_id=1, source_target_pairs={{0,28},{4,0},{8,4},{12,8},{16,12},{20,16},{24,20},{28,24},{1,29},{... | collective-permute-start | bytes 589832 | tf_op jit(solution)/shard_map/ppermute | solution.py:416
  32.8 2.9 %collective-permute-start.11 = (bf16[2,192,512]{2,1,0:T(8,128)(2,1)S(1)}, bf16[2,192,512]{2,1,0:T(8,128)(2,1)S(1)}, u32[]{:S(2)}, u32[]{:S(2)}) collective-permute-start(bf16[2,192,512]{2,1,0:T(8,128)(2,1)S(1)} %pad_maximum_fusion), channel_id=1, source_target_pairs={{0,128},{64,192},{128,0},{192,64},{1,129},{65,193},{129,1},{193,65... | collective-permute-start | bytes 1179656 | tf_op jit(solution)/shard_map/ppermute | solution.py:416
  36.5 5.0 %pose.1.cams_ref = f32[64,12]{1,0:T(8,128)} custom-call(f32[64,8,128]{2,1,0:T(8,128)} %copy-done.1, f32[1,1024]{1,0:T(1,128)} %bitcast.11, bf16[3,1024,512]{2,1,0:T(8,128)(2,1)} %qkv_ref.1, bf16[512,1024]{1,0:T(8,128)(2,1)} %out_ref.2, f32[12,1024]{1,0:T(8,128)} %bitcast.9), custom_call_target="tpu_custom_call" | custom-call | tf_op jit(solution)/shard_map/pose/pallas_call | solution.py:106
  41.5 2.5 %collective-permute-done.3.refs_6_ = bf16[192,512]{1,0:T(8,128)(2,1)S(1)} collective-permute-done((bf16[192,512]{1,0:T(8,128)(2,1)S(1)}, bf16[192,512]{1,0:T(8,128)(2,1)S(1)}, u32[]{:S(2)}, u32[]{:S(2)}) %collective-permute-start.3) | collective-permute-done | bytes 196640 | tf_op jit(solution)/shard_map/ppermute | solution.py:416
  45.9 2.5 %collective-permute-start.8 = (bf16[192,512]{1,0:T(8,128)(2,1)S(1)}, bf16[192,512]{1,0:T(8,128)(2,1)S(1)}, u32[]{:S(2)}, u32[]{:S(2)}) collective-permute-start(bf16[192,512]{1,0:T(8,128)(2,1)S(1)} %collective-permute-done.4.refs_8_), channel_id=1, source_target_pairs={{0,28},{4,0},{8,4},{12,8},{16,12},{20,16},{24,20},{28,24},{1,29},{... | collective-permute-start | bytes 589832 | tf_op jit(solution)/shard_map/ppermute | solution.py:416
  48.5 4.7 %collective-permute-done.7.refs_12_ = bf16[192,512]{1,0:T(8,128)(2,1)S(1)} collective-permute-done((bf16[192,512]{1,0:T(8,128)(2,1)S(1)}, bf16[192,512]{1,0:T(8,128)(2,1)S(1)}, u32[]{:S(2)}, u32[]{:S(2)}) %collective-permute-start.7) | collective-permute-done | bytes 196640 | tf_op jit(solution)/shard_map/ppermute | solution.py:416
  55.4 1.4 collective-permute-done.9.refs_20_
  59.4 1.7 %collective-permute-done.17.refs_13_ = bf16[192,512]{1,0:T(8,128)(2,1)S(1)} collective-permute-done((bf16[192,512]{1,0:T(8,128)(2,1)S(1)}, bf16[192,512]{1,0:T(8,128)(2,1)S(1)}, u32[]{:S(2)}, u32[]{:S(2)}) %collective-permute-start.17) | collective-permute-done | bytes 196640 | tf_op jit(solution)/shard_map/ppermute | solution.py:416
  62.4 14.4 %prep.1 = (bf16[1536,512]{1,0:T(8,128)(2,1)}, bf16[1536,512]{1,0:T(8,128)(2,1)}, bf16[8,192,512]{2,1,0:T(8,128)(2,1)}, bf16[192,512]{1,0:T(8,128)(2,1)}, f32[1,12]{1,0:T(1,128)}) custom-call(f32[64,12]{1,0:T(8,128)} %pose.1.cams_ref, f32[64,12]{1,0:T(8,128)} %copy-done.29, f32[6,1024]{1,0:T(8,128)} %embed_ref.1, f32[2,1,512]{2,1,0:T(1,128)} %bitcast.10, ...), custom_call_target="tpu_custom_call" | custom-call | tf_op jit(solution)/shard_map/prep/pallas_call | solution.py:267
  76.8 27.9 %attend.3 = bf16[4,208,512]{2,1,0:T(8,128)(2,1)} custom-call(bf16[8,192,512]{2,1,0:T(8,128)(2,1)} %get-tuple-element.52.q_ref, bf16[1536,512]{1,0:T(8,128)(2,1)} %get-tuple-element.50.k_ref, bf16[1536,512]{1,0:T(8,128)(2,1)} %get-tuple-element.51.v_ref), custom_call_target="tpu_custom_call" | custom-call | tf_op jit(solution)/shard_map/attend/pallas_call | solution.py:333
  104.7 3.5 %all-to-all-start.1 = ((bf16[4,208,512]{2,1,0:T(8,128)(2,1)}), bf16[4,208,512]{2,1,0:T(8,128)(2,1)S(1)}, u32[]{:S(2)}, u32[]{:S(2)}) async-start(bf16[4,208,512]{2,1,0:T(8,128)(2,1)} %attend.3), calls=%async_computation.1 | async-start | bytes 1703936 | tf_op jit(solution)/shard_map/all_to_all | solution.py:476
  108.2 11.7 %attend.5 = (bf16[1,208,512]{2,1,0:T(8,128)(2,1)}, bf16[1,208,512]{2,1,0:T(8,128)(2,1)}, bf16[1,208,512]{2,1,0:T(8,128)(2,1)}) custom-call(bf16[8,192,512]{2,1,0:T(8,128)(2,1)} %get-tuple-element.52.q_ref, bf16[1536,512]{1,0:T(8,128)(2,1)} %get-tuple-element.50.k_ref, bf16[1536,512]{1,0:T(8,128)(2,1)} %get-tuple-element.51.v_ref), custom_call_target="tpu_custom_call" | custom-call | tf_op jit(solution)/shard_map/attend/pallas_call | solution.py:333
  119.9 2.6 %collective-permute-start.24 = (bf16[1,208,512]{2,1,0:T(8,128)(2,1)}, bf16[1,208,512]{2,1,0:T(8,128)(2,1)S(1)}, u32[]{:S(2)}, u32[]{:S(2)}) collective-permute-start(bf16[1,208,512]{2,1,0:T(8,128)(2,1)} %get-tuple-element.54), channel_id=1, source_target_pairs={{0,192},{64,0},{128,64},{192,128},{1,193},{65,1},{129,65},{193,129... | collective-permute-start | bytes 638984 | tf_op jit(solution)/shard_map/ppermute | solution.py:416
  124.6 2.8 %join.1 = bf16[1,208,512]{2,1,0:T(8,128)(2,1)} custom-call(bf16[4,208,512]{2,1,0:T(8,128)(2,1)} %copy-done), custom_call_target="tpu_custom_call" | custom-call | tf_op jit(solution)/shard_map/join/pallas_call | solution.py:384
  127.4 1.8 %collective-permute-start.23 = (bf16[1,208,512]{2,1,0:T(8,128)(2,1)}, bf16[1,208,512]{2,1,0:T(8,128)(2,1)S(1)}, u32[]{:S(2)}, u32[]{:S(2)}) collective-permute-start(bf16[1,208,512]{2,1,0:T(8,128)(2,1)} %join.1), channel_id=1, source_target_pairs={{0,32},{32,0},{1,33},{33,1},{2,34},{34,2},{3,35},{35,3},{4,36},{36... | collective-permute-start | bytes 638984 | tf_op jit(solution)/shard_map/ppermute | solution.py:416
  129.3 6.0 %attend.4.refs_0_ = bf16[1,208,512]{2,1,0:T(8,128)(2,1)} custom-call(bf16[8,192,512]{2,1,0:T(8,128)(2,1)} %get-tuple-element.52.q_ref, bf16[1536,512]{1,0:T(8,128)(2,1)} %get-tuple-element.50.k_ref, bf16[1536,512]{1,0:T(8,128)(2,1)} %get-tuple-element.51.v_ref), custom_call_target="tpu_custom_call" | custom-call | tf_op jit(solution)/shard_map/attend/pallas_call | solution.py:333
  137.4 3.4 %merge.1 = (f32[192,512]{1,0:T(8,128)}, bf16[192,512]{1,0:T(8,128)(2,1)}) custom-call(bf16[512,1024]{1,0:T(8,128)(2,1)} %out_ref.3, bf16[1,208,512]{2,1,0:T(8,128)(2,1)} %attend.4.refs_0_, bf16[1,208,512]{2,1,0:T(8,128)(2,1)} %copy-done.12, bf16[1,208,512]{2,1,0:T(8,128)(2,1)} %copy-done.9, bf16[1,208,512]{2,1,0:T(8,128)(2,1)} %copy-done.10, ...), custom_call_target="tpu_custom_call" | custom-call | tf_op jit(solution)/shard_map/merge/pallas_call | solution.py:402
  141.9 1.3 collective-permute-done.27
  143.1 1.7 %add_convert_fusion = bf16[192,512]{1,0:T(8,128)(2,1)} fusion(f32[192,512]{1,0:T(8,128)} %get-tuple-element.57, bf16[192,512]{1,0:T(8,128)(2,1)S(1)} %collective-permute-done.27, bf16[192,512]{1,0:T(8,128)(2,1)S(1)} %copy-done.13), kind=kLoop, calls=%fused_computation.1 | loop fusion | flops 491520 | bytes 983040 | tf_op jit(solution)/shard_map/convert_element_type | solution.py:484
  (106 shorter events, 18.1 us)
Async XLA Ops:
  3.9 25.2 %all-to-all-start = ((f32[64,8,128]{2,1,0:T(8,128)}), f32[64,8,128]{2,1,0:T(8,128)S(1)}, u32[]{:S(2)}, u32[]{:S(2)}) async-start(f32[64,8,128]{2,1,0:T(8,128)} %get-tuple-element.31), calls=%async_computation | async-start | bytes 524288 | tf_op jit(solution)/shard_map/all_to_all | solution.py:444
  17.4 7.7 %collective-permute-start.2 = (bf16[192,512]{1,0:T(8,128)(2,1)}, bf16[192,512]{1,0:T(8,128)(2,1)S(1)}, u32[]{:S(2)}, u32[]{:S(2)}) collective-permute-start(bf16[192,512]{1,0:T(8,128)(2,1)} %get-tuple-element.32.refs_0_.refs_16_), channel_id=1, source_target_pairs={{0,32},{32,0},{1,33},{33,1},{2,34},{34,2},{3,35},{35,3},{4,36},{36... | collective-permute-start | bytes 589832 | tf_op jit(solution)/shard_map/ppermute | solution.py:416
  18.5 9.7 %collective-permute-start.1 = (bf16[192,512]{1,0:T(8,128)(2,1)}, bf16[192,512]{1,0:T(8,128)(2,1)S(1)}, u32[]{:S(2)}, u32[]{:S(2)}) collective-permute-start(bf16[192,512]{1,0:T(8,128)(2,1)} %get-tuple-element.32.refs_0_.refs_16_), channel_id=1, source_target_pairs={{0,28},{4,0},{8,4},{12,8},{16,12},{20,16},{24,20},{28,24},{1,29},{... | collective-permute-start | bytes 589832 | tf_op jit(solution)/shard_map/ppermute | solution.py:416
  20.9 8.2 %collective-permute-start = (bf16[192,512]{1,0:T(8,128)(2,1)}, bf16[192,512]{1,0:T(8,128)(2,1)S(1)}, u32[]{:S(2)}, u32[]{:S(2)}) collective-permute-start(bf16[192,512]{1,0:T(8,128)(2,1)} %get-tuple-element.32.refs_0_.refs_16_), channel_id=1, source_target_pairs={{0,4},{4,8},{8,12},{12,16},{16,20},{20,24},{24,28},{28,0},{1,5},{5... | collective-permute-start | bytes 589832 | tf_op jit(solution)/shard_map/ppermute | solution.py:416
  20.9 20.6 %collective-permute-start.5 = (bf16[192,512]{1,0:T(8,128)(2,1)}, bf16[192,512]{1,0:T(8,128)(2,1)S(1)}, u32[]{:S(2)}, u32[]{:S(2)}) collective-permute-start(bf16[192,512]{1,0:T(8,128)(2,1)} %get-tuple-element.32.refs_0_.refs_16_), channel_id=1, source_target_pairs={{0,16},{4,20},{8,24},{12,28},{16,0},{20,4},{24,8},{28,12},{1,17},{... | collective-permute-start | bytes 589832 | tf_op jit(solution)/shard_map/ppermute | solution.py:416
  29.1 14.9 %collective-permute-start.3 = (bf16[192,512]{1,0:T(8,128)(2,1)S(1)}, bf16[192,512]{1,0:T(8,128)(2,1)S(1)}, u32[]{:S(2)}, u32[]{:S(2)}) collective-permute-start(bf16[192,512]{1,0:T(8,128)(2,1)S(1)} %collective-permute-done.refs_2_), channel_id=1, source_target_pairs={{0,4},{4,8},{8,12},{12,16},{16,20},{20,24},{24,28},{28,0},{1,5},{5... | collective-permute-start | bytes 589832 | tf_op jit(solution)/shard_map/ppermute | solution.py:416
  30.3 13.8 %collective-permute-start.4 = (bf16[192,512]{1,0:T(8,128)(2,1)S(1)}, bf16[192,512]{1,0:T(8,128)(2,1)S(1)}, u32[]{:S(2)}, u32[]{:S(2)}) collective-permute-start(bf16[192,512]{1,0:T(8,128)(2,1)S(1)} %collective-permute-done.1.refs_4_), channel_id=1, source_target_pairs={{0,28},{4,0},{8,4},{12,8},{16,12},{20,16},{24,20},{28,24},{1,29},{... | collective-permute-start | bytes 589832 | tf_op jit(solution)/shard_map/ppermute | solution.py:416
  32.8 21.8 %collective-permute-start.11 = (bf16[2,192,512]{2,1,0:T(8,128)(2,1)S(1)}, bf16[2,192,512]{2,1,0:T(8,128)(2,1)S(1)}, u32[]{:S(2)}, u32[]{:S(2)}) collective-permute-start(bf16[2,192,512]{2,1,0:T(8,128)(2,1)S(1)} %pad_maximum_fusion), channel_id=1, source_target_pairs={{0,128},{64,192},{128,0},{192,64},{1,129},{65,193},{129,1},{193,65... | collective-permute-start | bytes 1179656 | tf_op jit(solution)/shard_map/ppermute | solution.py:416
  35.8 19.5 %collective-permute-start.10 = (bf16[2,192,512]{2,1,0:T(8,128)(2,1)S(1)}, bf16[2,192,512]{2,1,0:T(8,128)(2,1)S(1)}, u32[]{:S(2)}, u32[]{:S(2)}) collective-permute-start(bf16[2,192,512]{2,1,0:T(8,128)(2,1)S(1)} %pad_maximum_fusion), channel_id=1, source_target_pairs={{0,192},{64,0},{128,64},{192,128},{1,193},{65,1},{129,65},{193,129... | collective-permute-start | bytes 1179656 | tf_op jit(solution)/shard_map/ppermute | solution.py:416
  44.9 11.9 %collective-permute-start.9 = (bf16[2,192,512]{2,1,0:T(8,128)(2,1)S(1)}, bf16[2,192,512]{2,1,0:T(8,128)(2,1)S(1)}, u32[]{:S(2)}, u32[]{:S(2)}) collective-permute-start(bf16[2,192,512]{2,1,0:T(8,128)(2,1)S(1)} %pad_maximum_fusion), channel_id=1, source_target_pairs={{0,64},{64,128},{128,192},{192,0},{1,65},{65,129},{129,193},{193,1... | collective-permute-start | bytes 1179656 | tf_op jit(solution)/shard_map/ppermute | solution.py:416
  45.8 7.3 %collective-permute-start.7 = (bf16[192,512]{1,0:T(8,128)(2,1)S(1)}, bf16[192,512]{1,0:T(8,128)(2,1)S(1)}, u32[]{:S(2)}, u32[]{:S(2)}) collective-permute-start(bf16[192,512]{1,0:T(8,128)(2,1)S(1)} %collective-permute-done.3.refs_6_), channel_id=1, source_target_pairs={{0,4},{4,8},{8,12},{12,16},{16,20},{20,24},{24,28},{28,0},{1,5},{5... | collective-permute-start | bytes 589832 | tf_op jit(solution)/shard_map/ppermute | solution.py:416
  45.9 8.4 %collective-permute-start.8 = (bf16[192,512]{1,0:T(8,128)(2,1)S(1)}, bf16[192,512]{1,0:T(8,128)(2,1)S(1)}, u32[]{:S(2)}, u32[]{:S(2)}) collective-permute-start(bf16[192,512]{1,0:T(8,128)(2,1)S(1)} %collective-permute-done.4.refs_8_), channel_id=1, source_target_pairs={{0,28},{4,0},{8,4},{12,8},{16,12},{20,16},{24,20},{28,24},{1,29},{... | collective-permute-start | bytes 589832 | tf_op jit(solution)/shard_map/ppermute | solution.py:416
  53.1 4.5 %collective-permute-start.12 = (bf16[192,512]{1,0:T(8,128)(2,1)S(1)}, bf16[192,512]{1,0:T(8,128)(2,1)S(1)}, u32[]{:S(2)}, u32[]{:S(2)}) collective-permute-start(bf16[192,512]{1,0:T(8,128)(2,1)S(1)} %collective-permute-done.refs_2_), channel_id=1, source_target_pairs={{0,2},{2,0},{1,3},{3,1},{4,6},{6,4},{5,7},{7,5},{8,10},{10,8},{9,1... | collective-permute-start | bytes 589832 | tf_op jit(solution)/shard_map/ppermute | solution.py:416
  54.3 3.4 %collective-permute-start.13 = (bf16[192,512]{1,0:T(8,128)(2,1)S(1)}, bf16[192,512]{1,0:T(8,128)(2,1)S(1)}, u32[]{:S(2)}, u32[]{:S(2)}) collective-permute-start(bf16[192,512]{1,0:T(8,128)(2,1)S(1)} %collective-permute-done.1.refs_4_), channel_id=1, source_target_pairs={{0,2},{2,0},{1,3},{3,1},{4,6},{6,4},{5,7},{7,5},{8,10},{10,8},{9,1... | collective-permute-start | bytes 589832 | tf_op jit(solution)/shard_map/ppermute | solution.py:416
  54.7 3.5 %collective-permute-start.19 = (bf16[192,512]{1,0:T(8,128)(2,1)S(1)}, bf16[192,512]{1,0:T(8,128)(2,1)S(1)}, u32[]{:S(2)}, u32[]{:S(2)}) collective-permute-start(bf16[192,512]{1,0:T(8,128)(2,1)S(1)} %collective-permute-done.2.refs_18_), channel_id=1, source_target_pairs={{0,2},{2,0},{1,3},{3,1},{4,6},{6,4},{5,7},{7,5},{8,10},{10,8},{9,1... | collective-permute-start | bytes 589832 | tf_op jit(solution)/shard_map/ppermute | solution.py:416
  55.3 3.0 %collective-permute-start.16 = (bf16[192,512]{1,0:T(8,128)(2,1)S(1)}, bf16[192,512]{1,0:T(8,128)(2,1)S(1)}, u32[]{:S(2)}, u32[]{:S(2)}) collective-permute-start(bf16[192,512]{1,0:T(8,128)(2,1)S(1)} %collective-permute-done.5.refs_10_), channel_id=1, source_target_pairs={{0,2},{2,0},{1,3},{3,1},{4,6},{6,4},{5,7},{7,5},{8,10},{10,8},{9,1... | collective-permute-start | bytes 589832 | tf_op jit(solution)/shard_map/ppermute | solution.py:416
  57.7 3.6 %collective-permute-start.20 = (bf16[2,192,512]{2,1,0:T(8,128)(2,1)S(1)}, bf16[2,192,512]{2,1,0:T(8,128)(2,1)S(1)}, u32[]{:S(2)}, u32[]{:S(2)}) collective-permute-start(bf16[2,192,512]{2,1,0:T(8,128)(2,1)S(1)} %collective-permute-done.9.refs_20_), channel_id=1, source_target_pairs={{0,2},{2,0},{1,3},{3,1},{4,6},{6,4},{5,7},{7,5},{8,10},{10,8},{9,1... | collective-permute-start | bytes 1179656 | tf_op jit(solution)/shard_map/ppermute | solution.py:416
  58.2 3.2 %collective-permute-start.21 = (bf16[2,192,512]{2,1,0:T(8,128)(2,1)S(1)}, bf16[2,192,512]{2,1,0:T(8,128)(2,1)S(1)}, u32[]{:S(2)}, u32[]{:S(2)}) collective-permute-start(bf16[2,192,512]{2,1,0:T(8,128)(2,1)S(1)} %collective-permute-done.10.refs_22_), channel_id=1, source_target_pairs={{0,2},{2,0},{1,3},{3,1},{4,6},{6,4},{5,7},{7,5},{8,10},{10,8},{9,1... | collective-permute-start | bytes 1179656 | tf_op jit(solution)/shard_map/ppermute | solution.py:416
  58.3 3.1 %collective-permute-start.22 = (bf16[2,192,512]{2,1,0:T(8,128)(2,1)S(1)}, bf16[2,192,512]{2,1,0:T(8,128)(2,1)S(1)}, u32[]{:S(2)}, u32[]{:S(2)}) collective-permute-start(bf16[2,192,512]{2,1,0:T(8,128)(2,1)S(1)} %collective-permute-done.11.refs_24_), channel_id=1, source_target_pairs={{0,2},{2,0},{1,3},{3,1},{4,6},{6,4},{5,7},{7,5},{8,10},{10,8},{9,1... | collective-permute-start | bytes 1179656 | tf_op jit(solution)/shard_map/ppermute | solution.py:416
  104.7 19.0 %all-to-all-start.1 = ((bf16[4,208,512]{2,1,0:T(8,128)(2,1)}), bf16[4,208,512]{2,1,0:T(8,128)(2,1)S(1)}, u32[]{:S(2)}, u32[]{:S(2)}) async-start(bf16[4,208,512]{2,1,0:T(8,128)(2,1)} %attend.3), calls=%async_computation.1 | async-start | bytes 1703936 | tf_op jit(solution)/shard_map/all_to_all | solution.py:476
  119.9 15.3 %collective-permute-start.24 = (bf16[1,208,512]{2,1,0:T(8,128)(2,1)}, bf16[1,208,512]{2,1,0:T(8,128)(2,1)S(1)}, u32[]{:S(2)}, u32[]{:S(2)}) collective-permute-start(bf16[1,208,512]{2,1,0:T(8,128)(2,1)} %get-tuple-element.54), channel_id=1, source_target_pairs={{0,192},{64,0},{128,64},{192,128},{1,193},{65,1},{129,65},{193,129... | collective-permute-start | bytes 638984 | tf_op jit(solution)/shard_map/ppermute | solution.py:416
  122.6 12.7 %collective-permute-start.25 = (bf16[1,208,512]{2,1,0:T(8,128)(2,1)}, bf16[1,208,512]{2,1,0:T(8,128)(2,1)S(1)}, u32[]{:S(2)}, u32[]{:S(2)}) collective-permute-start(bf16[1,208,512]{2,1,0:T(8,128)(2,1)} %get-tuple-element.55), channel_id=1, source_target_pairs={{0,128},{64,192},{128,0},{192,64},{1,129},{65,193},{129,1},{193,65... | collective-permute-start | bytes 638984 | tf_op jit(solution)/shard_map/ppermute | solution.py:416
  123.1 12.9 %collective-permute-start.26 = (bf16[1,208,512]{2,1,0:T(8,128)(2,1)}, bf16[1,208,512]{2,1,0:T(8,128)(2,1)S(1)}, u32[]{:S(2)}, u32[]{:S(2)}) collective-permute-start(bf16[1,208,512]{2,1,0:T(8,128)(2,1)} %get-tuple-element.56), channel_id=1, source_target_pairs={{0,64},{64,128},{128,192},{192,0},{1,65},{65,129},{129,193},{193,1... | collective-permute-start | bytes 638984 | tf_op jit(solution)/shard_map/ppermute | solution.py:416
  127.4 8.6 %collective-permute-start.23 = (bf16[1,208,512]{2,1,0:T(8,128)(2,1)}, bf16[1,208,512]{2,1,0:T(8,128)(2,1)S(1)}, u32[]{:S(2)}, u32[]{:S(2)}) collective-permute-start(bf16[1,208,512]{2,1,0:T(8,128)(2,1)} %join.1), channel_id=1, source_target_pairs={{0,32},{32,0},{1,33},{33,1},{2,34},{34,2},{3,35},{35,3},{4,36},{36... | collective-permute-start | bytes 638984 | tf_op jit(solution)/shard_map/ppermute | solution.py:416
  (36 other events, 246.2 us)
where the time goes:
time: 148 us; the launch traced here: 145 us
  Pallas kernels  73.2 us (49%)
  starting transfers between devices  46.8 us (32%)
  waiting for transfers between devices  16.8 us (11%)
  local copies, waits for them, and re-layouts  3.19 us (2%)
  other arithmetic  2.71 us (2%)
  between operations  2.42 us (2%)
    pallas_call x3, Pallas kernels, attend(): pl.pallas_call(attend_kernel, grid=(spans,), in_specs=[pl.BlockSpec((pl.E...  45.6 us
    ppermute x28, starting transfers between devices, shift(): lax.ppermute(value, axis, [(at, (at + by) % size) for at in range(size)])  29.8 us
    ppermute x28, waiting for transfers between devices, shift(): lax.ppermute(value, axis, [(at, (at + by) % size) for at in range(size)])  16.8 us
    pallas_call x1, Pallas kernels, prep(): pl.pallas_call(functools.partial(prep_kernel, keys, queries, tuple(spots)...  14.4 us
    all_to_all x1, starting transfers between devices, local(): cam_all = lax.all_to_all(send, ('x', 'y', 'z'), 0, 0)  13.5 us
    pallas_call x1, Pallas kernels, pose(): pl.pallas_call(pose_kernel, out_shape=jax.ShapeDtypeStruct((FRAMES, CAM),...  4.98 us
    all_to_all x1, starting transfers between devices, local(): lax.all_to_all(attend(query, key, val, RING, 2, True)[0], 'x', 0, 0)  3.5 us
    pallas_call x1, Pallas kernels, merge(): pl.pallas_call(merge_kernel, in_specs=[VMEM] * (1 + len(parts)), out_spec...  3.43 us
  transfers between devices with their start and end apart: 30, of which 10 were waited for; matrix products, arithmetic and copies ran while one was open for 1% of the time, Pallas kernels for 18%

commit v1 on v0

--- a/solution.py
+++ b/solution.py
@@ -23,7 +23,8 @@
 CAM = 12
 FRAMES = 64
 LOG2E = 1.4426950408889634
-VMEM_LIMIT = 56 * 1024 * 1024
+MIB = 1024 * 1024
+VMEM_LIMIT = 56 * MIB
 SMEM = pl.BlockSpec(memory_space=pltpu.SMEM)
 VMEM = pl.BlockSpec(memory_space=pltpu.VMEM)
 
@@ -73,12 +74,19 @@
     )(order, mask, tokens)
 
 
-def pose_kernel(cam_ref, gain_ref, qkv_ref, out_ref, head_ref, cams_ref):
+def pose_kernel(cam_ref, gain_ref, qkv_hbm, out_hbm, head_ref, cams_ref, qkv_ref, out_ref, sems):
+    copies = [pltpu.make_async_copy(qkv_hbm.at[at], qkv_ref.at[at], sems.at[at]) for at in range(3)]
+    copies.append(pltpu.make_async_copy(out_hbm, out_ref, sems.at[3]))
+    for copy in copies:
+        copy.start()
     cam = jnp.concatenate([cam_ref[:, at, :] for at in range(8)], axis=1)
     mean = jnp.mean(cam * cam, axis=-1, keepdims=True)
     normed = (cam * lax.rsqrt(mean + 1e-06) * gain_ref[...]).astype(BF16)
+    copies[0].wait()
     query = mm(normed, qkv_ref[0]).astype(BF16)
+    copies[1].wait()
     keys = mm(normed, qkv_ref[1]).astype(BF16)
+    copies[2].wait()
     values = mm(normed, qkv_ref[2]).astype(BF16)
     lane_head = lax.broadcasted_iota(jnp.int32, (FRAMES, HALF), 1) >> 6
     stacked = jnp.concatenate(
@@ -92,6 +100,7 @@
     for head in range(HEADS):
         rows = mixed[head * FRAMES : (head + 1) * FRAMES]
         picked = rows if picked is None else jnp.where(lane_head == head, rows, picked)
+    copies[3].wait()
     partial = mm(picked.astype(BF16), out_ref[...]) + 0.5 * cam
     cams_ref[...] = lax.dot_general(
         partial,
@@ -105,6 +114,12 @@
 def pose(cam_all, pose_norm, pose_qkv, pose_out, camera_head):
     return pl.pallas_call(
         pose_kernel,
+        in_specs=[VMEM, VMEM] + [pl.BlockSpec(memory_space=pltpu.HBM)] * 2 + [VMEM],
+        scratch_shapes=[
+            pltpu.VMEM((3, WIDTH, HALF), BF16),
+            pltpu.VMEM((HALF, WIDTH), BF16),
+            pltpu.SemaphoreType.DMA((4,)),
+        ],
         out_shape=jax.ShapeDtypeStruct((FRAMES, CAM), F32),
         compiler_params=pltpu.CompilerParams(vmem_limit_bytes=VMEM_LIMIT),
         name="pose",
@@ -162,22 +177,29 @@
         copies.append(copy)
         return copy
 
-    matrices = ([1, 2] if keys else []) + ([0] if queries else [])
+    groups = list(keys) + list(queries)
+    firsts = [sum(len(group) for group in groups[:index]) for index in range(len(groups))]
+    waits = {}
+
+    def fetch_group(index):
+        for at in range(firsts[index], firsts[index] + len(groups[index])):
+            array, plane = spots[at]
+            pair = inputs[2 * array : 2 * array + 2]
+            if plane is not None:
+                pair = [ref.at[plane] for ref in pair]
+            waits[at] = [
+                fetch(ref, block_buf.at[at, :, pl.ds(side * HALF, HALF)]) for side, ref in enumerate(pair)
+            ]
+
+    fetch_group(0)
     weights = {
         which: [
             fetch(qkv_hbm.at[which, side], qkv_ref.at[which, pl.ds(at * HALF, HALF)])
             for at, side in enumerate((core, other))
         ]
-        for which in matrices
+        for which in (1, 2, 0)
     }
-    waits = []
-    for at, (array, plane) in enumerate(spots):
-        pair = inputs[2 * array : 2 * array + 2]
-        if plane is not None:
-            pair = [ref.at[plane] for ref in pair]
-        waits.append(
-            [fetch(ref, block_buf.at[at, :, pl.ds(side * HALF, HALF)]) for side, ref in enumerate(pair)]
-        )
+    fetch_group(1)
     row = lax.broadcasted_iota(jnp.int32, (2 * GROUP, FRAMES), 0)
     key_frame = at_x * 16 + at_y * 8 + ((at_z - row) & 7)
     query_frame = ((at_x - row) & 3) * 16 + ((at_y - (row >> 2)) & 1) * 8 + at_z
@@ -215,9 +237,11 @@
         return mm(rows, qkv_ref[which])
 
     own_ref[...] = cams[0:1]
-    at = 0
-    for group in list(keys) + list(queries):
+    for index, group in enumerate(groups):
+        at = firsts[index]
         members = range(at, at + len(group))
+        if index + 2 < len(groups):
+            fetch_group(index + 2)
         for member in members:
             for copy in waits[member]:
                 copy.wait()
@@ -244,7 +268,6 @@
                 held = at + spot - GROUP
                 q_ref[held] = query[spot * ROWS : (spot + 1) * ROWS]
                 send(q_ref.at[held], q_hbm.at[RING + ((at_x - by_x) & (RING - 1)) if by_y else by_x])
-        at += len(group)
     for copy in sent:
         copy.wait()
 
@@ -384,7 +407,7 @@
     return pl.pallas_call(
         join_kernel,
         out_shape=jax.ShapeDtypeStruct((1, TALL, HALF), BF16),
-        compiler_params=pltpu.CompilerParams(vmem_limit_bytes=VMEM_LIMIT),
+        compiler_params=pltpu.CompilerParams(vmem_limit_bytes=8 * MIB),
         name="join",
     )(parts)
 
@@ -407,7 +430,7 @@
             jax.ShapeDtypeStruct((ROWS, HALF), F32),
             jax.ShapeDtypeStruct((ROWS, HALF), BF16),
         ],
-        compiler_params=pltpu.CompilerParams(vmem_limit_bytes=VMEM_LIMIT),
+        compiler_params=pltpu.CompilerParams(vmem_limit_bytes=10 * MIB),
         name="merge",
     )(render_out, *parts)
 

time: 148 us -> 143 us (0.966)
  Pallas kernels: 73.2 us -> 68.1 us
  waiting for transfers between devices: 16.8 us -> 19.6 us
    ppermute x28, waiting for transfers between devices: 16.8 us -> 19.6 us  [shift(): lax.ppermute(value, axis, [(at, (at + by) % size) for at in range(size)])]
    pallas_call x1, Pallas kernels: 3.43 us -> 1.13 us  [merge(): pl.pallas_call(merge_kernel, in_specs=[VMEM] * (1 + len(parts)), out_spec...]
    pallas_call x1, Pallas kernels: 2.8 us -> 0.93 us  [join(): pl.pallas_call(join_kernel, out_shape=jax.ShapeDtypeStruct((1, TALL, HALF...]
    unnamed x60 -> x54, local copies, waits for them, and re-layouts: 3.19 us -> 1.9 us
  transfers between devices with their start and end apart: 30 -> 30, of which waited for: 10 -> 10; matrix products, arithmetic and copies ran while one was open for 1% -> 1% of each run, Pallas kernels for 18% -> 17%
where the time goes in v1:
time: 143 us; the launch traced here: 140 us
  Pallas kernels  68.1 us (48%)
  starting transfers between devices  46.1 us (32%)
  waiting for transfers between devices  19.6 us (14%)
  between operations  2.42 us (2%)
  local copies, waits for them, and re-layouts  1.9 us (1%)
  other arithmetic  1.71 us (1%)
    pallas_call x3, Pallas kernels, attend(): pl.pallas_call(attend_kernel, grid=(spans,), in_specs=[pl.BlockSpec((pl.E...  45.6 us
    ppermute x28, starting transfers between devices, shift(): lax.ppermute(value, axis, [(at, (at + by) % size) for at in range(size)])  29.1 us
    ppermute x28, waiting for transfers between devices, shift(): lax.ppermute(value, axis, [(at, (at + by) % size) for at in range(size)])  19.6 us
    all_to_all x1, starting transfers between devices, local(): cam_all = lax.all_to_all(send, ('x', 'y', 'z'), 0, 0)  13.5 us
    pallas_call x1, Pallas kernels, prep(): pl.pallas_call(functools.partial(prep_kernel, keys, queries, tuple(spots)...  13.2 us
    pallas_call x1, Pallas kernels, pose(): pl.pallas_call(pose_kernel, in_specs=[VMEM, VMEM] + [pl.BlockSpec(memory_...  5.21 us
    all_to_all x1, starting transfers between devices, local(): lax.all_to_all(attend(query, key, val, RING, 2, True)[0], 'x', 0, 0)  3.5 us
  transfers between devices with their start and end apart: 30, of which 10 were waited for; matrix products, arithmetic and copies ran while one was open for 1% of the time, Pallas kernels for 17%

profile of v1, /device:TPU:1, one launch (start us, length us, event | category | flops | bytes accessed | tf_op | source)
XLA Modules:
  0.0 139.8 jit_solution(3148800855552411723)
XLA Ops:
  1.9 2.0 %start.1 = (f32[64,8,128]{2,1,0:T(8,128)}, bf16[192,512]{1,0:T(8,128)(2,1)}, bf16[192,512]{1,0:T(8,128)(2,1)}) custom-call(s32[1]{0:T(128)S(6)} %copy.13.order_ref, s32[1]{0:T(128)S(6)} %copy.14.mask_ref, bf16[192,1024]{1,0:T(8,128)(2,1)} %tokens_ref.1), custom_call_target="tpu_custom_call" | custom-call | tf_op jit(solution)/shard_map/start/pallas_call | solution.py:63
  3.9 13.5 %all-to-all-start = ((f32[64,8,128]{2,1,0:T(8,128)}), f32[64,8,128]{2,1,0:T(8,128)S(1)}, u32[]{:S(2)}, u32[]{:S(2)}) async-start(f32[64,8,128]{2,1,0:T(8,128)} %get-tuple-element.31), calls=%async_computation | async-start | bytes 524288 | tf_op jit(solution)/shard_map/all_to_all | solution.py:467
  18.5 2.4 %collective-permute-start.1 = (bf16[192,512]{1,0:T(8,128)(2,1)}, bf16[192,512]{1,0:T(8,128)(2,1)S(1)}, u32[]{:S(2)}, u32[]{:S(2)}) collective-permute-start(bf16[192,512]{1,0:T(8,128)(2,1)} %get-tuple-element.32.refs_0_.refs_16_), channel_id=1, source_target_pairs={{0,28},{4,0},{8,4},{12,8},{16,12},{20,16},{24,20},{28,24},{1,29},{... | collective-permute-start | bytes 589832 | tf_op jit(solution)/shard_map/ppermute | solution.py:439
  20.9 4.2 %collective-permute-start.5 = (bf16[192,512]{1,0:T(8,128)(2,1)}, bf16[192,512]{1,0:T(8,128)(2,1)S(1)}, u32[]{:S(2)}, u32[]{:S(2)}) collective-permute-start(bf16[192,512]{1,0:T(8,128)(2,1)} %get-tuple-element.32.refs_0_.refs_16_), channel_id=1, source_target_pairs={{0,16},{4,20},{8,24},{12,28},{16,0},{20,4},{24,8},{28,12},{1,17},{... | collective-permute-start | bytes 589832 | tf_op jit(solution)/shard_map/ppermute | solution.py:439
  25.1 3.1 %collective-permute-done.1.refs_4_ = bf16[192,512]{1,0:T(8,128)(2,1)S(1)} collective-permute-done((bf16[192,512]{1,0:T(8,128)(2,1)}, bf16[192,512]{1,0:T(8,128)(2,1)S(1)}, u32[]{:S(2)}, u32[]{:S(2)}) %collective-permute-start.1) | collective-permute-done | bytes 196640 | tf_op jit(solution)/shard_map/ppermute | solution.py:439
  29.1 1.1 collective-permute-start.3
  30.3 1.6 %collective-permute-start.4 = (bf16[192,512]{1,0:T(8,128)(2,1)S(1)}, bf16[192,512]{1,0:T(8,128)(2,1)S(1)}, u32[]{:S(2)}, u32[]{:S(2)}) collective-permute-start(bf16[192,512]{1,0:T(8,128)(2,1)S(1)} %collective-permute-done.1.refs_4_), channel_id=1, source_target_pairs={{0,28},{4,0},{8,4},{12,8},{16,12},{20,16},{24,20},{28,24},{1,29},{... | collective-permute-start | bytes 589832 | tf_op jit(solution)/shard_map/ppermute | solution.py:439
  32.8 2.9 %collective-permute-start.11 = (bf16[2,192,512]{2,1,0:T(8,128)(2,1)S(1)}, bf16[2,192,512]{2,1,0:T(8,128)(2,1)S(1)}, u32[]{:S(2)}, u32[]{:S(2)}) collective-permute-start(bf16[2,192,512]{2,1,0:T(8,128)(2,1)S(1)} %pad_maximum_fusion), channel_id=1, source_target_pairs={{0,128},{64,192},{128,0},{192,64},{1,129},{65,193},{129,1},{193,65... | collective-permute-start | bytes 1179656 | tf_op jit(solution)/shard_map/ppermute | solution.py:439
  36.5 5.2 %pose.1.cams_ref = f32[64,12]{1,0:T(8,128)} custom-call(f32[64,8,128]{2,1,0:T(8,128)} %copy-done.2, f32[1,1024]{1,0:T(1,128)} %bitcast.11, bf16[3,1024,512]{2,1,0:T(8,128)(2,1)} %qkv_hbm.1, bf16[512,1024]{1,0:T(8,128)(2,1)} %out_hbm.1, f32[12,1024]{1,0:T(8,128)} %bitcast.9), custom_call_target="tpu_custom_call" | custom-call | tf_op jit(solution)/shard_map/pose/pallas_call | solution.py:115
  41.8 2.2 %collective-permute-done.3.refs_6_ = bf16[192,512]{1,0:T(8,128)(2,1)S(1)} collective-permute-done((bf16[192,512]{1,0:T(8,128)(2,1)S(1)}, bf16[192,512]{1,0:T(8,128)(2,1)S(1)}, u32[]{:S(2)}, u32[]{:S(2)}) %collective-permute-start.3) | collective-permute-done | bytes 196640 | tf_op jit(solution)/shard_map/ppermute | solution.py:439
  46.2 2.3 %collective-permute-start.8 = (bf16[192,512]{1,0:T(8,128)(2,1)S(1)}, bf16[192,512]{1,0:T(8,128)(2,1)S(1)}, u32[]{:S(2)}, u32[]{:S(2)}) collective-permute-start(bf16[192,512]{1,0:T(8,128)(2,1)S(1)} %collective-permute-done.4.refs_8_), channel_id=1, source_target_pairs={{0,28},{4,0},{8,4},{12,8},{16,12},{20,16},{24,20},{28,24},{1,29},{... | collective-permute-start | bytes 589832 | tf_op jit(solution)/shard_map/ppermute | solution.py:439
  48.5 4.7 %collective-permute-done.7.refs_12_ = bf16[192,512]{1,0:T(8,128)(2,1)S(1)} collective-permute-done((bf16[192,512]{1,0:T(8,128)(2,1)S(1)}, bf16[192,512]{1,0:T(8,128)(2,1)S(1)}, u32[]{:S(2)}, u32[]{:S(2)}) %collective-permute-start.7) | collective-permute-done | bytes 196640 | tf_op jit(solution)/shard_map/ppermute | solution.py:439
  53.1 1.2 collective-permute-start.12
  55.4 1.6 %collective-permute-done.9.refs_20_ = bf16[2,192,512]{2,1,0:T(8,128)(2,1)S(1)} collective-permute-done((bf16[2,192,512]{2,1,0:T(8,128)(2,1)S(1)}, bf16[2,192,512]{2,1,0:T(8,128)(2,1)S(1)}, u32[]{:S(2)}, u32[]{:S(2)}) %collective-permute-start.9) | collective-permute-done | bytes 393248 | tf_op jit(solution)/shard_map/ppermute | solution.py:439
  59.6 1.7 %collective-permute-done.17.refs_13_ = bf16[192,512]{1,0:T(8,128)(2,1)S(1)} collective-permute-done((bf16[192,512]{1,0:T(8,128)(2,1)S(1)}, bf16[192,512]{1,0:T(8,128)(2,1)S(1)}, u32[]{:S(2)}, u32[]{:S(2)}) %collective-permute-start.17) | collective-permute-done | bytes 196640 | tf_op jit(solution)/shard_map/ppermute | solution.py:439
  62.7 13.2 %prep.1 = (bf16[1536,512]{1,0:T(8,128)(2,1)}, bf16[1536,512]{1,0:T(8,128)(2,1)}, bf16[8,192,512]{2,1,0:T(8,128)(2,1)}, bf16[192,512]{1,0:T(8,128)(2,1)}, f32[1,12]{1,0:T(1,128)}) custom-call(f32[64,12]{1,0:T(8,128)} %pose.1.cams_ref, f32[64,12]{1,0:T(8,128)} %copy-done.26, f32[6,1024]{1,0:T(8,128)} %embed_ref.1, f32[2,1,512]{2,1,0:T(1,128)} %bitcast.10, ...), custom_call_target="tpu_custom_call" | custom-call | tf_op jit(solution)/shard_map/prep/pallas_call | solution.py:290
  75.9 27.9 %attend.3 = bf16[4,208,512]{2,1,0:T(8,128)(2,1)} custom-call(bf16[8,192,512]{2,1,0:T(8,128)(2,1)} %get-tuple-element.52.q_ref, bf16[1536,512]{1,0:T(8,128)(2,1)} %get-tuple-element.50.k_ref, bf16[1536,512]{1,0:T(8,128)(2,1)} %get-tuple-element.51.v_ref), custom_call_target="tpu_custom_call" | custom-call | tf_op jit(solution)/shard_map/attend/pallas_call | solution.py:356
  103.8 3.5 %all-to-all-start.1 = ((bf16[4,208,512]{2,1,0:T(8,128)(2,1)}), bf16[4,208,512]{2,1,0:T(8,128)(2,1)S(1)}, u32[]{:S(2)}, u32[]{:S(2)}) async-start(bf16[4,208,512]{2,1,0:T(8,128)(2,1)} %attend.3), calls=%async_computation.1 | async-start | bytes 1703936 | tf_op jit(solution)/shard_map/all_to_all | solution.py:499
  107.3 11.7 %attend.5 = (bf16[1,208,512]{2,1,0:T(8,128)(2,1)}, bf16[1,208,512]{2,1,0:T(8,128)(2,1)}, bf16[1,208,512]{2,1,0:T(8,128)(2,1)}) custom-call(bf16[8,192,512]{2,1,0:T(8,128)(2,1)} %get-tuple-element.52.q_ref, bf16[1536,512]{1,0:T(8,128)(2,1)} %get-tuple-element.50.k_ref, bf16[1536,512]{1,0:T(8,128)(2,1)} %get-tuple-element.51.v_ref), custom_call_target="tpu_custom_call" | custom-call | tf_op jit(solution)/shard_map/attend/pallas_call | solution.py:356
  119.0 2.6 %collective-permute-start.24 = (bf16[1,208,512]{2,1,0:T(8,128)(2,1)}, bf16[1,208,512]{2,1,0:T(8,128)(2,1)S(1)}, u32[]{:S(2)}, u32[]{:S(2)}) collective-permute-start(bf16[1,208,512]{2,1,0:T(8,128)(2,1)} %get-tuple-element.54), channel_id=1, source_target_pairs={{0,192},{64,0},{128,64},{192,128},{1,193},{65,1},{129,65},{193,129... | collective-permute-start | bytes 638984 | tf_op jit(solution)/shard_map/ppermute | solution.py:439
  123.8 1.9 %collective-permute-start.23 = (bf16[1,208,512]{2,1,0:T(8,128)(2,1)S(1)}, bf16[1,208,512]{2,1,0:T(8,128)(2,1)S(1)}, u32[]{:S(2)}, u32[]{:S(2)}) collective-permute-start(bf16[1,208,512]{2,1,0:T(8,128)(2,1)S(1)} %join.1), channel_id=1, source_target_pairs={{0,32},{32,0},{1,33},{33,1},{2,34},{34,2},{3,35},{35,3},{4,36},{36... | collective-permute-start | bytes 638984 | tf_op jit(solution)/shard_map/ppermute | solution.py:439
  125.6 6.0 %attend.4.refs_0_ = bf16[1,208,512]{2,1,0:T(8,128)(2,1)} custom-call(bf16[8,192,512]{2,1,0:T(8,128)(2,1)} %get-tuple-element.52.q_ref, bf16[1536,512]{1,0:T(8,128)(2,1)} %get-tuple-element.50.k_ref, bf16[1536,512]{1,0:T(8,128)(2,1)} %get-tuple-element.51.v_ref), custom_call_target="tpu_custom_call" | custom-call | tf_op jit(solution)/shard_map/attend/pallas_call | solution.py:356
  131.6 3.5 %collective-permute-done.26.refs_4_ = bf16[1,208,512]{2,1,0:T(8,128)(2,1)S(1)} collective-permute-done((bf16[1,208,512]{2,1,0:T(8,128)(2,1)}, bf16[1,208,512]{2,1,0:T(8,128)(2,1)S(1)}, u32[]{:S(2)}, u32[]{:S(2)}) %collective-permute-start.26) | collective-permute-done | bytes 213024 | tf_op jit(solution)/shard_map/ppermute | solution.py:439
  136.1 1.1 merge.1
  (100 shorter events, 16.3 us)
Async XLA Ops:
  3.9 25.2 %all-to-all-start = ((f32[64,8,128]{2,1,0:T(8,128)}), f32[64,8,128]{2,1,0:T(8,128)S(1)}, u32[]{:S(2)}, u32[]{:S(2)}) async-start(f32[64,8,128]{2,1,0:T(8,128)} %get-tuple-element.31), calls=%async_computation | async-start | bytes 524288 | tf_op jit(solution)/shard_map/all_to_all | solution.py:467
  17.4 7.7 %collective-permute-start.2 = (bf16[192,512]{1,0:T(8,128)(2,1)}, bf16[192,512]{1,0:T(8,128)(2,1)S(1)}, u32[]{:S(2)}, u32[]{:S(2)}) collective-permute-start(bf16[192,512]{1,0:T(8,128)(2,1)} %get-tuple-element.32.refs_0_.refs_16_), channel_id=1, source_target_pairs={{0,32},{32,0},{1,33},{33,1},{2,34},{34,2},{3,35},{35,3},{4,36},{36... | collective-permute-start | bytes 589832 | tf_op jit(solution)/shard_map/ppermute | solution.py:439
  18.5 9.7 %collective-permute-start.1 = (bf16[192,512]{1,0:T(8,128)(2,1)}, bf16[192,512]{1,0:T(8,128)(2,1)S(1)}, u32[]{:S(2)}, u32[]{:S(2)}) collective-permute-start(bf16[192,512]{1,0:T(8,128)(2,1)} %get-tuple-element.32.refs_0_.refs_16_), channel_id=1, source_target_pairs={{0,28},{4,0},{8,4},{12,8},{16,12},{20,16},{24,20},{28,24},{1,29},{... | collective-permute-start | bytes 589832 | tf_op jit(solution)/shard_map/ppermute | solution.py:439
  20.9 8.2 %collective-permute-start = (bf16[192,512]{1,0:T(8,128)(2,1)}, bf16[192,512]{1,0:T(8,128)(2,1)S(1)}, u32[]{:S(2)}, u32[]{:S(2)}) collective-permute-start(bf16[192,512]{1,0:T(8,128)(2,1)} %get-tuple-element.32.refs_0_.refs_16_), channel_id=1, source_target_pairs={{0,4},{4,8},{8,12},{12,16},{16,20},{20,24},{24,28},{28,0},{1,5},{5... | collective-permute-start | bytes 589832 | tf_op jit(solution)/shard_map/ppermute | solution.py:439
  20.9 20.9 %collective-permute-start.5 = (bf16[192,512]{1,0:T(8,128)(2,1)}, bf16[192,512]{1,0:T(8,128)(2,1)S(1)}, u32[]{:S(2)}, u32[]{:S(2)}) collective-permute-start(bf16[192,512]{1,0:T(8,128)(2,1)} %get-tuple-element.32.refs_0_.refs_16_), channel_id=1, source_target_pairs={{0,16},{4,20},{8,24},{12,28},{16,0},{20,4},{24,8},{28,12},{1,17},{... | collective-permute-start | bytes 589832 | tf_op jit(solution)/shard_map/ppermute | solution.py:439
  29.1 14.9 %collective-permute-start.3 = (bf16[192,512]{1,0:T(8,128)(2,1)S(1)}, bf16[192,512]{1,0:T(8,128)(2,1)S(1)}, u32[]{:S(2)}, u32[]{:S(2)}) collective-permute-start(bf16[192,512]{1,0:T(8,128)(2,1)S(1)} %collective-permute-done.refs_2_), channel_id=1, source_target_pairs={{0,4},{4,8},{8,12},{12,16},{16,20},{20,24},{24,28},{28,0},{1,5},{5... | collective-permute-start | bytes 589832 | tf_op jit(solution)/shard_map/ppermute | solution.py:439
  30.3 13.8 %collective-permute-start.4 = (bf16[192,512]{1,0:T(8,128)(2,1)S(1)}, bf16[192,512]{1,0:T(8,128)(2,1)S(1)}, u32[]{:S(2)}, u32[]{:S(2)}) collective-permute-start(bf16[192,512]{1,0:T(8,128)(2,1)S(1)} %collective-permute-done.1.refs_4_), channel_id=1, source_target_pairs={{0,28},{4,0},{8,4},{12,8},{16,12},{20,16},{24,20},{28,24},{1,29},{... | collective-permute-start | bytes 589832 | tf_op jit(solution)/shard_map/ppermute | solution.py:439
  32.8 21.8 %collective-permute-start.11 = (bf16[2,192,512]{2,1,0:T(8,128)(2,1)S(1)}, bf16[2,192,512]{2,1,0:T(8,128)(2,1)S(1)}, u32[]{:S(2)}, u32[]{:S(2)}) collective-permute-start(bf16[2,192,512]{2,1,0:T(8,128)(2,1)S(1)} %pad_maximum_fusion), channel_id=1, source_target_pairs={{0,128},{64,192},{128,0},{192,64},{1,129},{65,193},{129,1},{193,65... | collective-permute-start | bytes 1179656 | tf_op jit(solution)/shard_map/ppermute | solution.py:439
  35.8 19.5 %collective-permute-start.10 = (bf16[2,192,512]{2,1,0:T(8,128)(2,1)S(1)}, bf16[2,192,512]{2,1,0:T(8,128)(2,1)S(1)}, u32[]{:S(2)}, u32[]{:S(2)}) collective-permute-start(bf16[2,192,512]{2,1,0:T(8,128)(2,1)S(1)} %pad_maximum_fusion), channel_id=1, source_target_pairs={{0,192},{64,0},{128,64},{192,128},{1,193},{65,1},{129,65},{193,129... | collective-permute-start | bytes 1179656 | tf_op jit(solution)/shard_map/ppermute | solution.py:439
  45.1 11.9 %collective-permute-start.9 = (bf16[2,192,512]{2,1,0:T(8,128)(2,1)S(1)}, bf16[2,192,512]{2,1,0:T(8,128)(2,1)S(1)}, u32[]{:S(2)}, u32[]{:S(2)}) collective-permute-start(bf16[2,192,512]{2,1,0:T(8,128)(2,1)S(1)} %pad_maximum_fusion), channel_id=1, source_target_pairs={{0,64},{64,128},{128,192},{192,0},{1,65},{65,129},{129,193},{193,1... | collective-permute-start | bytes 1179656 | tf_op jit(solution)/shard_map/ppermute | solution.py:439
  45.8 7.3 %collective-permute-start.7 = (bf16[192,512]{1,0:T(8,128)(2,1)S(1)}, bf16[192,512]{1,0:T(8,128)(2,1)S(1)}, u32[]{:S(2)}, u32[]{:S(2)}) collective-permute-start(bf16[192,512]{1,0:T(8,128)(2,1)S(1)} %collective-permute-done.3.refs_6_), channel_id=1, source_target_pairs={{0,4},{4,8},{8,12},{12,16},{16,20},{20,24},{24,28},{28,0},{1,5},{5... | collective-permute-start | bytes 589832 | tf_op jit(solution)/shard_map/ppermute | solution.py:439
  46.2 8.1 %collective-permute-start.8 = (bf16[192,512]{1,0:T(8,128)(2,1)S(1)}, bf16[192,512]{1,0:T(8,128)(2,1)S(1)}, u32[]{:S(2)}, u32[]{:S(2)}) collective-permute-start(bf16[192,512]{1,0:T(8,128)(2,1)S(1)} %collective-permute-done.4.refs_8_), channel_id=1, source_target_pairs={{0,28},{4,0},{8,4},{12,8},{16,12},{20,16},{24,20},{28,24},{1,29},{... | collective-permute-start | bytes 589832 | tf_op jit(solution)/shard_map/ppermute | solution.py:439
  53.1 4.8 %collective-permute-start.12 = (bf16[192,512]{1,0:T(8,128)(2,1)S(1)}, bf16[192,512]{1,0:T(8,128)(2,1)S(1)}, u32[]{:S(2)}, u32[]{:S(2)}) collective-permute-start(bf16[192,512]{1,0:T(8,128)(2,1)S(1)} %collective-permute-done.refs_2_), channel_id=1, source_target_pairs={{0,2},{2,0},{1,3},{3,1},{4,6},{6,4},{5,7},{7,5},{8,10},{10,8},{9,1... | collective-permute-start | bytes 589832 | tf_op jit(solution)/shard_map/ppermute | solution.py:439
  54.3 3.7 %collective-permute-start.13 = (bf16[192,512]{1,0:T(8,128)(2,1)S(1)}, bf16[192,512]{1,0:T(8,128)(2,1)S(1)}, u32[]{:S(2)}, u32[]{:S(2)}) collective-permute-start(bf16[192,512]{1,0:T(8,128)(2,1)S(1)} %collective-permute-done.1.refs_4_), channel_id=1, source_target_pairs={{0,2},{2,0},{1,3},{3,1},{4,6},{6,4},{5,7},{7,5},{8,10},{10,8},{9,1... | collective-permute-start | bytes 589832 | tf_op jit(solution)/shard_map/ppermute | solution.py:439
  54.7 3.7 %collective-permute-start.19 = (bf16[192,512]{1,0:T(8,128)(2,1)S(1)}, bf16[192,512]{1,0:T(8,128)(2,1)S(1)}, u32[]{:S(2)}, u32[]{:S(2)}) collective-permute-start(bf16[192,512]{1,0:T(8,128)(2,1)S(1)} %collective-permute-done.2.refs_18_), channel_id=1, source_target_pairs={{0,2},{2,0},{1,3},{3,1},{4,6},{6,4},{5,7},{7,5},{8,10},{10,8},{9,1... | collective-permute-start | bytes 589832 | tf_op jit(solution)/shard_map/ppermute | solution.py:439
  55.3 3.3 %collective-permute-start.16 = (bf16[192,512]{1,0:T(8,128)(2,1)S(1)}, bf16[192,512]{1,0:T(8,128)(2,1)S(1)}, u32[]{:S(2)}, u32[]{:S(2)}) collective-permute-start(bf16[192,512]{1,0:T(8,128)(2,1)S(1)} %collective-permute-done.5.refs_10_), channel_id=1, source_target_pairs={{0,2},{2,0},{1,3},{3,1},{4,6},{6,4},{5,7},{7,5},{8,10},{10,8},{9,1... | collective-permute-start | bytes 589832 | tf_op jit(solution)/shard_map/ppermute | solution.py:439
  58.0 3.6 %collective-permute-start.20 = (bf16[2,192,512]{2,1,0:T(8,128)(2,1)S(1)}, bf16[2,192,512]{2,1,0:T(8,128)(2,1)S(1)}, u32[]{:S(2)}, u32[]{:S(2)}) collective-permute-start(bf16[2,192,512]{2,1,0:T(8,128)(2,1)S(1)} %collective-permute-done.9.refs_20_), channel_id=1, source_target_pairs={{0,2},{2,0},{1,3},{3,1},{4,6},{6,4},{5,7},{7,5},{8,10},{10,8},{9,1... | collective-permute-start | bytes 1179656 | tf_op jit(solution)/shard_map/ppermute | solution.py:439
  58.4 3.2 %collective-permute-start.21 = (bf16[2,192,512]{2,1,0:T(8,128)(2,1)S(1)}, bf16[2,192,512]{2,1,0:T(8,128)(2,1)S(1)}, u32[]{:S(2)}, u32[]{:S(2)}) collective-permute-start(bf16[2,192,512]{2,1,0:T(8,128)(2,1)S(1)} %collective-permute-done.10.refs_22_), channel_id=1, source_target_pairs={{0,2},{2,0},{1,3},{3,1},{4,6},{6,4},{5,7},{7,5},{8,10},{10,8},{9,1... | collective-permute-start | bytes 1179656 | tf_op jit(solution)/shard_map/ppermute | solution.py:439
  58.5 3.1 %collective-permute-start.22 = (bf16[2,192,512]{2,1,0:T(8,128)(2,1)S(1)}, bf16[2,192,512]{2,1,0:T(8,128)(2,1)S(1)}, u32[]{:S(2)}, u32[]{:S(2)}) collective-permute-start(bf16[2,192,512]{2,1,0:T(8,128)(2,1)S(1)} %collective-permute-done.11.refs_24_), channel_id=1, source_target_pairs={{0,2},{2,0},{1,3},{3,1},{4,6},{6,4},{5,7},{7,5},{8,10},{10,8},{9,1... | collective-permute-start | bytes 1179656 | tf_op jit(solution)/shard_map/ppermute | solution.py:439
  103.8 19.0 %all-to-all-start.1 = ((bf16[4,208,512]{2,1,0:T(8,128)(2,1)}), bf16[4,208,512]{2,1,0:T(8,128)(2,1)S(1)}, u32[]{:S(2)}, u32[]{:S(2)}) async-start(bf16[4,208,512]{2,1,0:T(8,128)(2,1)} %attend.3), calls=%async_computation.1 | async-start | bytes 1703936 | tf_op jit(solution)/shard_map/all_to_all | solution.py:499
  119.0 12.6 %collective-permute-start.24 = (bf16[1,208,512]{2,1,0:T(8,128)(2,1)}, bf16[1,208,512]{2,1,0:T(8,128)(2,1)S(1)}, u32[]{:S(2)}, u32[]{:S(2)}) collective-permute-start(bf16[1,208,512]{2,1,0:T(8,128)(2,1)} %get-tuple-element.54), channel_id=1, source_target_pairs={{0,192},{64,0},{128,64},{192,128},{1,193},{65,1},{129,65},{193,129... | collective-permute-start | bytes 638984 | tf_op jit(solution)/shard_map/ppermute | solution.py:439
  121.7 10.0 %collective-permute-start.25 = (bf16[1,208,512]{2,1,0:T(8,128)(2,1)}, bf16[1,208,512]{2,1,0:T(8,128)(2,1)S(1)}, u32[]{:S(2)}, u32[]{:S(2)}) collective-permute-start(bf16[1,208,512]{2,1,0:T(8,128)(2,1)} %get-tuple-element.55), channel_id=1, source_target_pairs={{0,128},{64,192},{128,0},{192,64},{1,129},{65,193},{129,1},{193,65... | collective-permute-start | bytes 638984 | tf_op jit(solution)/shard_map/ppermute | solution.py:439
  122.2 12.9 %collective-permute-start.26 = (bf16[1,208,512]{2,1,0:T(8,128)(2,1)}, bf16[1,208,512]{2,1,0:T(8,128)(2,1)S(1)}, u32[]{:S(2)}, u32[]{:S(2)}) collective-permute-start(bf16[1,208,512]{2,1,0:T(8,128)(2,1)} %get-tuple-element.56), channel_id=1, source_target_pairs={{0,64},{64,128},{128,192},{192,0},{1,65},{65,129},{129,193},{193,1... | collective-permute-start | bytes 638984 | tf_op jit(solution)/shard_map/ppermute | solution.py:439
  123.8 11.4 %collective-permute-start.23 = (bf16[1,208,512]{2,1,0:T(8,128)(2,1)S(1)}, bf16[1,208,512]{2,1,0:T(8,128)(2,1)S(1)}, u32[]{:S(2)}, u32[]{:S(2)}) collective-permute-start(bf16[1,208,512]{2,1,0:T(8,128)(2,1)S(1)} %join.1), channel_id=1, source_target_pairs={{0,32},{32,0},{1,33},{33,1},{2,34},{34,2},{3,35},{35,3},{4,36},{36... | collective-permute-start | bytes 638984 | tf_op jit(solution)/shard_map/ppermute | solution.py:439
  (33 other events, 261.5 us)
